TPU v7x, 32 devices: a whole 2x2x4 slice. The times are simulated.
32 devices in a mesh: kr: 16 (over z, y, x), kc: 2 (over core).
Axes of the slice: x: 2, y: 2, z: 4, core: 2. Of those that a mesh axis runs over, the one named last changes fastest.
Arguments:
- pair_conduction: bfloat16 [384, 64, 4096], P('kr', None, 'kc'), may hold values from -6 to 6
- pair_valence: bfloat16 [384, 64, 4096], P('kr', None, 'kc'), may hold values from -6 to 6
- screened: bfloat16 [16, 4096, 4096], P('kr', 'kc'), may hold values from -0.09375 to 0.09375
- sphere_sizes: int32 [16], replicated, may hold values from 2048 to 4096
Outputs:
- kernels: float32 [384, 64, 64], P('kr', 'kc')
All inputs are finite; a program needn't handle non-finite values.
Results may differ from a plain program's by a relative error of at most 0.0029.
Values may be sent and summed in bfloat16 or wider, within the bound.
A program may use at most 128 MiB of HBM per device.

v0:
```python
import jax
import jax.numpy as jnp
from jax import lax
from jax.sharding import PartitionSpec as P

prefactor = 0.015625


def from_behind(value, axis, steps):
    count = lax.axis_size(axis)
    pairs = [(source, (source + steps) % count) for source in range(count)]
    return lax.ppermute(value, axis, pairs)


def restrict(slab, sphere, first_row):
    slab_rows = slab.shape[0]
    gvectors = slab.shape[1]
    row_inside = first_row + jnp.arange(slab_rows, dtype=jnp.int32) < sphere
    col_inside = jnp.arange(gvectors, dtype=jnp.int32) < sphere
    keep = row_inside[:, None] & col_inside[None, :]
    return jnp.where(keep, slab, jnp.zeros((), slab.dtype))


def shards(pair_conduction, pair_valence, screened, sphere_sizes):
    slab_rows = screened.shape[1]
    group_size = pair_valence.shape[0] // 3
    owner_index = lax.axis_index("kr")
    first_row = lax.axis_index("kc") * slab_rows
    own_slab = restrict(screened[0], sphere_sizes[owner_index], first_row)
    slabs = (own_slab, own_slab, own_slab)
    from_upper = from_behind(
        (pair_conduction[group_size : 2 * group_size], pair_valence[group_size : 2 * group_size]),
        "kr",
        -1,
    )
    from_lower = from_behind(
        (pair_conduction[2 * group_size :], pair_valence[2 * group_size :]), "kr", 1
    )
    conduction = jnp.concatenate([pair_conduction[:group_size], from_upper[0], from_lower[0]], 0)
    valence = jnp.concatenate([pair_valence[:group_size], from_upper[1], from_lower[1]], 0)
    portion = lax.all_gather(valence, "kc", axis=2, tiled=True)
    products = []
    for group_index in range(3):
        columns = slabs[group_index]
        group_block = portion[group_index * group_size : (group_index + 1) * group_size]
        products.append(
            lax.dot_general(
                group_block, columns, (((2,), (1,)), ((), ())), preferred_element_type=jnp.float32
            )
        )
    applied = jnp.concatenate(products, 0).astype(jnp.bfloat16)
    partial_value = jnp.einsum(
        "pag,pbg->pab", conduction, applied, preferred_element_type=jnp.float32
    )
    kernels = lax.psum_scatter(partial_value, "kc", scatter_dimension=1, tiled=True) * prefactor
    back_upper = from_behind(kernels[group_size : 2 * group_size], "kr", 1)
    back_lower = from_behind(kernels[2 * group_size :], "kr", -1)
    kernels = jnp.concatenate([kernels[:group_size], back_upper, back_lower], 0)
    return kernels


def solution(mesh):
    return jax.shard_map(
        shards,
        mesh=mesh,
        in_specs=(P("kr", None, "kc"), P("kr", None, "kc"), P("kr", "kc", None), P()),
        out_specs=P("kr", "kc", None),
        check_vma=False,
    )
```

profile of v0, /device:TPU:0, one launch (start us, length us, event | category | flops | bytes accessed | tf_op | source)
XLA Modules:
  0.0 244.7 jit_solution(15140062757617967446)
XLA Ops:
  6.5 0.0 all-gather.2.cloned.1.call-start
  6.5 4.0 %fusion.16 = (bf16[8,64,2048]{2,1,0:T(8,128)(2,1)S(1)}, bf16[8,64,2048]{2,1,0:T(8,128)(2,1)S(1)}, bf16[8,64,2048]{2,1,0:T(8,128)(2,1)S(1)}) fusion(bf16[24,64,2048]{2,1,0:T(8,128)(2,1)} %param.5), kind=kLoop, calls=%fused_computation.22 | loop fusion | bytes 12582912 | tf_op jit(solution)/shard_map/slice | solution.py:40
  10.5 7.0 %collective-permute-start.2 = (bf16[8,64,2048]{2,1,0:T(8,128)(2,1)S(1)}, bf16[8,64,2048]{2,1,0:T(8,128)(2,1)S(1)}, u32[]{:S(2)}, u32[]{:S(2)}) collective-permute-start(bf16[8,64,2048]{2,1,0:T(8,128)(2,1)S(1)} %get-tuple-element.7), channel_id=1, source_target_pairs={{0,30},{2,0},{4,2},{6,4},{8,6},{10,8},{12,10},{14,12},{16,14},{18,... | collective-permute-start | bytes 6291464 | tf_op jit(solution)/shard_map/ppermute | solution.py:12
  17.5 0.0 collective-permute-start.3
  17.5 44.9 %collective-permute-done.2 = bf16[8,64,2048]{2,1,0:T(8,128)(2,1)S(1)} collective-permute-done((bf16[8,64,2048]{2,1,0:T(8,128)(2,1)S(1)}, bf16[8,64,2048]{2,1,0:T(8,128)(2,1)S(1)}, u32[]{:S(2)}, u32[]{:S(2)}) %collective-permute-start.2) | collective-permute-done | bytes 2097184 | tf_op jit(solution)/shard_map/ppermute | solution.py:12
  62.4 42.8 %collective-permute-done.3 = bf16[8,64,2048]{2,1,0:T(8,128)(2,1)S(1)} collective-permute-done((bf16[8,64,2048]{2,1,0:T(8,128)(2,1)S(1)}, bf16[8,64,2048]{2,1,0:T(8,128)(2,1)S(1)}, u32[]{:S(2)}, u32[]{:S(2)}) %collective-permute-start.3) | collective-permute-done | bytes 2097184 | tf_op jit(solution)/shard_map/ppermute | solution.py:12
  105.2 5.0 %pad_maximum_fusion = bf16[24,64,2048]{2,1,0:T(8,128)(2,1)} fusion(bf16[8,64,2048]{2,1,0:T(8,128)(2,1)S(1)} %collective-permute-done.3, bf16[8,64,2048]{2,1,0:T(8,128)(2,1)S(1)} %collective-permute-done.2, bf16[8,64,2048]{2,1,0:T(8,128)(2,1)S(1)} %get-tuple-element.5), kind=kLoop, calls=%fused_computation.8 | loop fusion | flops 6291456 | bytes 12582912 | tf_op jit(solution)/shard_map/concatenate | solution.py:40
  110.2 0.0 all-gather.2.cloned.1.call-update
  110.2 0.0 copy-start
  110.2 0.0 reduce-scatter.2.cloned.1.call-start
  110.2 5.8 %fusion.17 = (bf16[8,64,2048]{2,1,0:T(8,128)(2,1)S(1)}, bf16[8,64,2048]{2,1,0:T(8,128)(2,1)}, bf16[8,64,2048]{2,1,0:T(8,128)(2,1)}) fusion(bf16[24,64,2048]{2,1,0:T(8,128)(2,1)} %param.4), kind=kLoop, calls=%fused_computation.23 | loop fusion | bytes 12582912 | tf_op jit(solution)/shard_map/slice | solution.py:39
  116.1 4.6 %collective-permute-start = (bf16[8,64,2048]{2,1,0:T(8,128)(2,1)}, bf16[8,64,2048]{2,1,0:T(8,128)(2,1)}, u32[]{:S(2)}, u32[]{:S(2)}) collective-permute-start(bf16[8,64,2048]{2,1,0:T(8,128)(2,1)} %get-tuple-element.10), channel_id=1, source_target_pairs={{0,30},{2,0},{4,2},{6,4},{8,6},{10,8},{12,10},{14,12},{16,14},{18,... | collective-permute-start | bytes 6291464 | tf_op jit(solution)/shard_map/ppermute | solution.py:12
  120.6 0.0 collective-permute-start.1
  120.6 0.0 copy-done
  120.6 0.6 dynamic_slice.3
  121.2 0.7 add_compare_fusion
  121.9 0.7 iota_compare_fusion
  122.6 13.0 %all-gather.2.cloned.1.call-done = bf16[24,64,4096]{2,1,0:T(8,128)(2,1)} async-done(((bf16[24,64,2048]{2,1,0:T(8,128)(2,1)}), bf16[24,64,4096]{2,1,0:T(8,128)(2,1)}) %all-gather.2.cloned.1.call-update) | async-done | bytes 12582928 | tf_op jit(solution)/shard_map/all_gather | solution.py:41
  135.6 13.8 %convolution_convert_fusion.1 = bf16[8,64,2048]{2,1,0:T(8,128)(2,1)S(1)} fusion(bf16[24,64,4096]{2,1,0:T(8,128)(2,1)} %all-gather.2.cloned.1.call-done, bf16[1,2048,4096]{2,1,0:T(8,128)(2,1)} %param.6, pred[4096]{0:T(1024)(128)(4,1)S(1)} %iota_compare_fusion, pred[2048]{0:T(1024)(128)(4,1)S(1)} %add_compare_fusion), kind=kOutput, calls=%fused_computation.15 | convolution fusion | flops 8607760384 | bytes 31463424 | tf_op jit(solution)/shard_map/dot_general | solution.py:47
  149.4 13.8 %convolution_convert_fusion.2 = bf16[8,64,2048]{2,1,0:T(8,128)(2,1)S(1)} fusion(bf16[24,64,4096]{2,1,0:T(8,128)(2,1)} %all-gather.2.cloned.1.call-done, bf16[1,2048,4096]{2,1,0:T(8,128)(2,1)} %param.6, pred[4096]{0:T(1024)(128)(4,1)S(1)} %iota_compare_fusion, pred[2048]{0:T(1024)(128)(4,1)S(1)} %add_compare_fusion), kind=kOutput, calls=%fused_computation.16 | convolution fusion | flops 8607760384 | bytes 31463424 | tf_op jit(solution)/shard_map/dot_general | solution.py:47
  163.2 14.0 %convolution_convert_fusion = bf16[8,64,2048]{2,1,0:T(8,128)(2,1)S(1)} fusion(bf16[24,64,4096]{2,1,0:T(8,128)(2,1)} %all-gather.2.cloned.1.call-done, bf16[1,2048,4096]{2,1,0:T(8,128)(2,1)} %param.6, pred[4096]{0:T(1024)(128)(4,1)S(1)} %iota_compare_fusion, pred[2048]{0:T(1024)(128)(4,1)S(1)} %add_compare_fusion), kind=kOutput, calls=%fused_computation.14 | convolution fusion | flops 8607760384 | bytes 31463424 | tf_op jit(solution)/shard_map/dot_general | solution.py:47
  177.2 0.0 collective-permute-done
  177.2 30.5 %collective-permute-done.1 = bf16[8,64,2048]{2,1,0:T(8,128)(2,1)} collective-permute-done((bf16[8,64,2048]{2,1,0:T(8,128)(2,1)}, bf16[8,64,2048]{2,1,0:T(8,128)(2,1)}, u32[]{:S(2)}, u32[]{:S(2)}) %collective-permute-start.1) | collective-permute-done | bytes 2097184 | tf_op jit(solution)/shard_map/ppermute | solution.py:12
  207.8 8.9 %fusion.1 = f32[24,64,64]{2,1,0:T(8,128)} fusion(bf16[8,64,2048]{2,1,0:T(8,128)(2,1)} %collective-permute-done.1, bf16[8,64,2048]{2,1,0:T(8,128)(2,1)} %collective-permute-done, bf16[8,64,2048]{2,1,0:T(8,128)(2,1)S(1)} %get-tuple-element.8, bf16[8,64,2048]{2,1,0:T(8,128)(2,1)S(1)} %convolution_convert_fusion, ...), kind=kOutput, calls=%fused_computation.2 | convolution fusion | flops 415236096 | bytes 12976128 | tf_op jit(solution)/shard_map/pag,pbg->pab/dot_general | solution.py:52
  216.7 0.0 reduce-scatter.2.cloned.1.call-update
  216.7 9.6 %reduce-scatter.2.cloned.1.call-done = f32[24,32,64]{2,1,0:T(8,128)} async-done(((f32[24,64,64]{2,1,0:T(8,128)}), f32[24,32,64]{2,1,0:T(8,128)}) %reduce-scatter.2.cloned.1.call-update) | async-done | bytes 196624 | tf_op jit(solution)/shard_map/reduce_scatter | solution.py:55
  226.3 1.0 broadcast_multiply_fusion
  227.4 1.8 collective-permute-start.4
  229.2 3.9 %collective-permute-start.5 = (f32[8,32,64]{2,1,0:T(8,128)S(1)}, f32[8,32,64]{2,1,0:T(8,128)S(1)}, u32[]{:S(2)}, u32[]{:S(2)}) collective-permute-start(f32[8,32,64]{2,1,0:T(8,128)S(1)} %get-tuple-element.12), channel_id=1, source_target_pairs={{0,30},{2,0},{4,2},{6,4},{8,6},{10,8},{12,10},{14,12},{16,14},{18,... | collective-permute-start | bytes 196616 | tf_op jit(solution)/shard_map/ppermute | solution.py:12
  233.1 3.9 %collective-permute-done.4 = f32[8,32,64]{2,1,0:T(8,128)S(1)} collective-permute-done((f32[8,32,64]{2,1,0:T(8,128)S(1)}, f32[8,32,64]{2,1,0:T(8,128)S(1)}, u32[]{:S(2)}, u32[]{:S(2)}) %collective-permute-start.4) | collective-permute-done | bytes 65568 | tf_op jit(solution)/shard_map/ppermute | solution.py:12
  236.9 0.2 collective-permute-done.5
  237.1 0.8 pad_maximum_fusion.1
  (1 shorter events, 0.0 us)
Async XLA Ops:
  6.5 129.0 %all-gather.2.cloned.1.call-start = ((), (), s32[]{:S(2)}) async-start(), calls=%async_computation.1 | async-start | bytes 18874368 | tf_op jit(solution)/shard_map/all_gather | solution.py:41
  10.5 51.9 %collective-permute-start.2 = (bf16[8,64,2048]{2,1,0:T(8,128)(2,1)S(1)}, bf16[8,64,2048]{2,1,0:T(8,128)(2,1)S(1)}, u32[]{:S(2)}, u32[]{:S(2)}) collective-permute-start(bf16[8,64,2048]{2,1,0:T(8,128)(2,1)S(1)} %get-tuple-element.7), channel_id=1, source_target_pairs={{0,30},{2,0},{4,2},{6,4},{8,6},{10,8},{12,10},{14,12},{16,14},{18,... | collective-permute-start | bytes 6291464 | tf_op jit(solution)/shard_map/ppermute | solution.py:12
  17.5 87.7 %collective-permute-start.3 = (bf16[8,64,2048]{2,1,0:T(8,128)(2,1)S(1)}, bf16[8,64,2048]{2,1,0:T(8,128)(2,1)S(1)}, u32[]{:S(2)}, u32[]{:S(2)}) collective-permute-start(bf16[8,64,2048]{2,1,0:T(8,128)(2,1)S(1)} %get-tuple-element.6), channel_id=1, source_target_pairs={{0,2},{2,4},{4,6},{6,8},{8,10},{10,12},{12,14},{14,16},{16,18},{18... | collective-permute-start | bytes 6291464 | tf_op jit(solution)/shard_map/ppermute | solution.py:12
  110.2 10.5 %copy-start = (s32[16]{0:T(128)S(1)}, s32[16]{0:T(128)}, u32[]{:S(2)}) copy-start(s32[16]{0:T(128)} %param.7) | copy-start | bytes 196
  110.2 116.1 %reduce-scatter.2.cloned.1.call-start = ((), (), s32[]{:S(2)}) async-start(), calls=%async_computation.2 | async-start | bytes 1179648 | tf_op jit(solution)/shard_map/reduce_scatter | solution.py:55
  116.1 61.2 %collective-permute-start = (bf16[8,64,2048]{2,1,0:T(8,128)(2,1)}, bf16[8,64,2048]{2,1,0:T(8,128)(2,1)}, u32[]{:S(2)}, u32[]{:S(2)}) collective-permute-start(bf16[8,64,2048]{2,1,0:T(8,128)(2,1)} %get-tuple-element.10), channel_id=1, source_target_pairs={{0,30},{2,0},{4,2},{6,4},{8,6},{10,8},{12,10},{14,12},{16,14},{18,... | collective-permute-start | bytes 6291464 | tf_op jit(solution)/shard_map/ppermute | solution.py:12
  120.6 87.1 %collective-permute-start.1 = (bf16[8,64,2048]{2,1,0:T(8,128)(2,1)}, bf16[8,64,2048]{2,1,0:T(8,128)(2,1)}, u32[]{:S(2)}, u32[]{:S(2)}) collective-permute-start(bf16[8,64,2048]{2,1,0:T(8,128)(2,1)} %get-tuple-element.9), channel_id=1, source_target_pairs={{0,2},{2,4},{4,6},{6,8},{8,10},{10,12},{12,14},{14,16},{16,18},{18... | collective-permute-start | bytes 6291464 | tf_op jit(solution)/shard_map/ppermute | solution.py:12
  227.4 9.5 %collective-permute-start.4 = (f32[8,32,64]{2,1,0:T(8,128)S(1)}, f32[8,32,64]{2,1,0:T(8,128)S(1)}, u32[]{:S(2)}, u32[]{:S(2)}) collective-permute-start(f32[8,32,64]{2,1,0:T(8,128)S(1)} %get-tuple-element.13), channel_id=1, source_target_pairs={{0,2},{2,4},{4,6},{6,8},{8,10},{10,12},{12,14},{14,16},{16,18},{18... | collective-permute-start | bytes 196616 | tf_op jit(solution)/shard_map/ppermute | solution.py:12
  229.2 8.0 %collective-permute-start.5 = (f32[8,32,64]{2,1,0:T(8,128)S(1)}, f32[8,32,64]{2,1,0:T(8,128)S(1)}, u32[]{:S(2)}, u32[]{:S(2)}) collective-permute-start(f32[8,32,64]{2,1,0:T(8,128)S(1)} %get-tuple-element.12), channel_id=1, source_target_pairs={{0,30},{2,0},{4,2},{6,4},{8,6},{10,8},{12,10},{14,12},{16,14},{18,... | collective-permute-start | bytes 196616 | tf_op jit(solution)/shard_map/ppermute | solution.py:12
Sparse Core Ops, SparseCore 0:
  110.3 25.2 all-gather.1
  216.8 9.4 reduce-scatter.1
where the time goes:
time: 245 us
  waiting for transfers between devices  145 us (59%)
  matrix products  50.5 us (21%)
  starting transfers between devices  17.3 us (7%)
  between operations  13.5 us (6%)
  local copies, waits for them, and re-layouts  10.4 us (4%)
  other arithmetic  8.1 us (3%)
    ppermute x6, waiting for transfers between devices, from_behind(): return lax.ppermute(value, axis, pairs)  122 us
    dot_general x3, matrix products, shards(): lax.dot_general(group_block, columns, (((2,), (1,)), ((), ())), preferred...  41.6 us
    ppermute x6, starting transfers between devices, from_behind(): return lax.ppermute(value, axis, pairs)  17.2 us
    all_gather x1, waiting for transfers between devices, shards(): portion = lax.all_gather(valence, 'kc', axis=2, tiled=True)  13 us
    reduce_scatter x1, waiting for transfers between devices, shards(): lax.psum_scatter(partial_value, 'kc', scatter_dimension=1, tiled=True)  9.63 us
    dot_general x1, matrix products, shards(): jnp.einsum('pag,pbg->pab', conduction, applied, preferred_element_type=jn...  8.89 us
    slice x1, local copies, waits for them, and re-layouts, shards(): pair_conduction[:group_size]  5.83 us
    concatenate x1, other arithmetic, shards(): jnp.concatenate([pair_valence[:group_size], from_upper[1], from_lower[1]]...  4.97 us
  transfers between devices with their start and end apart: 8, of which 7 were waited for; matrix products, arithmetic and copies ran while one was open for 20% of the time, Pallas kernels for 0%

commit v1 on v0

v1 whole, which is shorter than its diff:
```python
import functools

import jax
import jax.numpy as jnp
from jax import lax
from jax.experimental import pallas as pl
from jax.experimental.pallas import tpu as pltpu
from jax.sharding import PartitionSpec as P

prefactor = 0.015625
over_last = (((1,), (1,)), ((), ()))


def at(index, size):
    return pl.ds(pl.multiple_of(index * size, size), size)


def kernel(
    owners, shares, cuts, bands,
    sizes, conduction_hbm, valence_hbm, screened_hbm, out,
    screened, conduction, valence, applied, returned, partial, others,
    load_sem, go_send, go_recv, share_send, share_recv, back_send, back_recv,
    sum_send, sum_recv,
):
    owner = lax.axis_index("kr")
    me = lax.axis_index("kc")
    neighbours = (lax.rem(owner + owners - 1, owners), lax.rem(owner + 1, owners))
    slab = screened.shape[0]
    group_rows = valence.shape[1] // 3
    rows = group_rows // cuts
    pairs = rows // bands
    out_rows = out.shape[1]
    tile = min(256, slab)

    def peer(step):
        return lax.rem(me + step, shares)

    def behind(step):
        return lax.rem(me + shares - step, shares)

    def piece(side, k):
        return (side + 1) * cuts + k

    def go(side, k):
        j = piece(side, k)
        return pltpu.make_async_remote_copy(
            src_ref=valence_hbm.at[at(j, rows)],
            dst_ref=valence.at[me, at(j, rows)],
            send_sem=go_send.at[side, k],
            recv_sem=go_recv.at[side, k],
            device_id={"kr": neighbours[side]},
            device_id_type=pl.DeviceIdType.MESH,
        )

    def share(step, j, source, sender):
        return pltpu.make_async_remote_copy(
            src_ref=source,
            dst_ref=valence.at[sender, at(j, rows)],
            send_sem=share_send.at[step - 1, j],
            recv_sem=share_recv.at[step - 1, j],
            device_id={"kc": peer(step)},
            device_id_type=pl.DeviceIdType.MESH,
        )

    def share_own(step, k):
        return share(step, k, valence_hbm.at[at(k, rows)], me)

    def share_piece(step, j):
        return share(step, j, valence.at[me, at(j, rows)], me)

    def shared(step, j):
        return share(step, j, valence.at[me, at(j, rows)], behind(step))

    def back(side, k):
        j = piece(side, k)
        return pltpu.make_async_remote_copy(
            src_ref=applied.at[at(j, rows)],
            dst_ref=returned.at[at(j - cuts, rows)],
            send_sem=back_send.at[side, k],
            recv_sem=back_recv.at[side, k],
            device_id={"kr": neighbours[1 - side]},
            device_id_type=pl.DeviceIdType.MESH,
        )

    def summand(step, j):
        return pltpu.make_async_remote_copy(
            src_ref=partial.at[at(j, pairs), at(peer(step), out_rows)],
            dst_ref=others.at[step - 1, at(j, pairs)],
            send_sem=sum_send.at[step - 1, j],
            recv_sem=sum_recv.at[step - 1, j],
            device_id={"kc": peer(step)},
            device_id_type=pl.DeviceIdType.MESH,
        )

    def apply(j):
        block = at(j, rows)

        def one(t, carry):
            total = jnp.zeros((rows, tile), jnp.float32)
            for part in range(shares):
                total += lax.dot_general(
                    valence[part, block],
                    screened[at(t, tile), part * slab : (part + 1) * slab],
                    over_last,
                    preferred_element_type=jnp.float32,
                )
            row = me * slab + t * tile + lax.broadcasted_iota(jnp.int32, (rows, tile), 1)
            total = jnp.where(row < sphere, total, 0.0)
            applied[block, at(t, tile)] = total.astype(applied.dtype)
            return carry

        lax.fori_loop(0, slab // tile, one, 0)

    def contract(j, source, k):
        product = lax.dot_general(
            conduction[at(j, rows)], source[at(k, rows)], over_last,
            preferred_element_type=jnp.float32,
        )
        for p in range(pairs):
            band = slice(p * bands, (p + 1) * bands)
            partial[j * pairs + p] = product[band, band]
        for step in range(1, shares):
            summand(step, j).start()

    barrier = pltpu.get_barrier_semaphore()
    for neighbour in neighbours:
        pl.semaphore_signal(
            barrier, inc=1, device_id={"kr": neighbour}, device_id_type=pl.DeviceIdType.MESH
        )
    for step in range(1, shares):
        pl.semaphore_signal(
            barrier, inc=1, device_id={"kc": peer(step)}, device_id_type=pl.DeviceIdType.MESH
        )
    load_screened = pltpu.make_async_copy(screened_hbm, screened, load_sem.at[0])
    load_valence = pltpu.make_async_copy(
        valence_hbm.at[pl.ds(0, group_rows)], valence.at[me, pl.ds(0, group_rows)], load_sem.at[1]
    )
    load_conduction = pltpu.make_async_copy(conduction_hbm, conduction, load_sem.at[2])
    pl.semaphore_wait(barrier, 2 + shares - 1)

    for k in range(cuts):
        for side in range(2):
            go(side, k).start()
    load_screened.start()
    load_valence.start()
    for k in range(cuts):
        for step in range(1, shares):
            share_own(step, k).start()
    load_conduction.start()

    sphere = sizes[owner]
    inside = lax.broadcasted_iota(jnp.int32, (1, screened.shape[1]), 1) < sphere
    keep = jnp.where(inside, 1.0, 0.0).astype(screened.dtype)
    load_screened.wait()
    strip = 64

    def mask(t, carry):
        screened[at(t, strip)] = screened[at(t, strip)] * keep
        return carry

    lax.fori_loop(0, slab // strip, mask, 0)
    load_valence.wait()
    load_conduction.wait()

    def own(k, carry):
        for step in range(1, shares):
            shared(step, k).wait_recv()
        apply(k)
        contract(k, applied, k)
        return carry

    lax.fori_loop(0, cuts, own, 0)

    def finish(k):
        for side in range(2):
            back(side, k).wait()
            contract(piece(side, k), returned, piece(side, k) - cuts)

    def travelling(k, carry):
        for side in range(2):
            go(side, k).wait_recv()
            for step in range(1, shares):
                share_piece(step, piece(side, k)).start()
        for side in range(2):
            j = piece(side, k)
            for step in range(1, shares):
                shared(step, j).wait_recv()
            apply(j)
            back(side, k).start()

        @pl.when(k > 0)
        def _():
            finish(k - 1)

        return carry

    lax.fori_loop(0, cuts, travelling, 0)
    finish(cuts - 1)

    def drain(j, carry):
        for step in range(1, shares):
            share_piece(step, j).wait_send()
            summand(step, j).wait()
        for p in range(pairs):
            pair = j * pairs + p
            total = partial[pair, at(me, out_rows)]
            for step in range(1, shares):
                total += others[step - 1, pair]
            out[pair] = total * prefactor
        return carry

    lax.fori_loop(0, 3 * cuts, drain, 0)
    for k in range(cuts):
        for side in range(2):
            go(side, k).wait_send()


def shards(owners, shares, pair_conduction, pair_valence, screened, sphere_sizes):
    count, bands, slab = pair_valence.shape
    gvectors = screened.shape[2]
    cuts = 4
    out_rows = pair_conduction.shape[1] // shares
    rows = count * bands
    dtype = pair_valence.dtype
    dma = pltpu.SemaphoreType.DMA
    anywhere = pl.BlockSpec(memory_space=pl.ANY)
    return pl.pallas_call(
        functools.partial(kernel, owners, shares, cuts, bands),
        out_shape=jax.ShapeDtypeStruct((count, out_rows, bands), jnp.float32),
        in_specs=[pl.BlockSpec(memory_space=pltpu.SMEM), anywhere, anywhere, anywhere],
        out_specs=pl.BlockSpec(memory_space=pltpu.VMEM),
        scratch_shapes=[
            pltpu.VMEM((slab, gvectors), dtype),
            pltpu.VMEM((rows, slab), dtype),
            pltpu.VMEM((shares, rows, slab), dtype),
            pltpu.VMEM((rows, slab), dtype),
            pltpu.VMEM((rows // 3 * 2, slab), dtype),
            pltpu.VMEM((count, bands, bands), jnp.float32),
            pltpu.VMEM((shares - 1, count, out_rows, bands), jnp.float32),
            dma((3,)),
            dma((2, cuts)),
            dma((2, cuts)),
            dma((shares - 1, 3 * cuts)),
            dma((shares - 1, 3 * cuts)),
            dma((2, cuts)),
            dma((2, cuts)),
            dma((shares - 1, 3 * cuts)),
            dma((shares - 1, 3 * cuts)),
        ],
        compiler_params=pltpu.CompilerParams(
            collective_id=0, has_side_effects=True, vmem_limit_bytes=58 * 1024 * 1024
        ),
        cost_estimate=pl.CostEstimate(
            flops=2 * rows * slab * gvectors + 2 * rows * bands * slab,
            bytes_accessed=2 * (2 * rows * slab + slab * gvectors),
            transcendentals=0,
        ),
    )(
        sphere_sizes,
        pair_conduction.reshape(rows, slab),
        pair_valence.reshape(rows, slab),
        screened.reshape(slab, gvectors),
    )


def solution(mesh):
    return jax.shard_map(
        functools.partial(shards, mesh.shape["kr"], mesh.shape["kc"]),
        mesh=mesh,
        in_specs=(P("kr", None, "kc"), P("kr", None, "kc"), P("kr", "kc", None), P()),
        out_specs=P("kr", "kc", None),
        check_vma=False,
    )
```

time: 245 us -> 192 us (0.78)
  Pallas kernels: 0 us -> 190 us
  waiting for transfers between devices: 145 us -> 0 us
  matrix products: 50.5 us -> 0 us
  starting transfers between devices: 17.3 us -> 0 us
  between operations: 13.5 us -> 0.01 us
  local copies, waits for them, and re-layouts: 10.4 us -> 1.77 us
  other arithmetic: 8.1 us -> 0 us
    pallas_call x0 -> x1, Pallas kernels: none -> 190 us  [shards(): pl.pallas_call(functools.partial(kernel, owners, shares, cuts, bands), ou...]
    ppermute x6 -> x0, waiting for transfers between devices: 122 us -> none  [from_behind(): return lax.ppermute(value, axis, pairs)]
    dot_general x4 -> x0, matrix products: 50.5 us -> none  [the longest x3 41.6 us: shards(): lax.dot_general(group_block, columns, (((2,), (1,)), ((), ())), preferred...]
    ppermute x6 -> x0, starting transfers between devices: 17.2 us -> none  [from_behind(): return lax.ppermute(value, axis, pairs)]
    all_gather x1 -> x0, waiting for transfers between devices: 13 us -> none  [shards(): portion = lax.all_gather(valence, 'kc', axis=2, tiled=True)]
    slice x3 -> x0, local copies, waits for them, and re-layouts: 9.82 us -> none  [the longest x1 5.83 us: shards(): pair_conduction[:group_size]]
    reduce_scatter x1 -> x0, waiting for transfers between devices: 9.63 us -> none  [shards(): lax.psum_scatter(partial_value, 'kc', scatter_dimension=1, tiled=True)]
    concatenate x2 -> x0, other arithmetic: 5.75 us -> none  [the longest x1 4.97 us: shards(): jnp.concatenate([pair_valence[:group_size], from_upper[1], from_lower[1]]...]
  transfers between devices with their start and end apart: 8 -> 0, of which waited for: 7 -> 0; matrix products, arithmetic and copies ran while one was open for 20% -> 0% of each run, Pallas kernels for 0% -> 0%
where the time goes in v1:
time: 192 us
  Pallas kernels  190 us (99%)
    pallas_call x1, Pallas kernels, shards(): pl.pallas_call(functools.partial(kernel, owners, shares, cuts, bands), ou...  190 us

profile of v1, /device:TPU:0, one launch (start us, length us, event | category | flops | bytes accessed | tf_op | source)
XLA Modules:
  0.0 191.7 jit_solution(10718329273412586297)
XLA Ops:
  0.0 190.0 %shard_map.46 = f32[24,32,64]{2,1,0:T(8,128)} custom-call(s32[16]{0:T(128)} %sizes.1, bf16[1536,2048]{1,0:T(8,128)(2,1)} %bitcast.4, bf16[1536,2048]{1,0:T(8,128)(2,1)} %bitcast.5, bf16[2048,4096]{1,0:T(8,128)(2,1)} %bitcast.3), custom_call_target="tpu_custom_call" | custom-call | flops 26172456960 | bytes 29360128 | tf_op jit(solution)/shard_map/pallas_call | solution.py:227
  190.0 1.8 copy.6

commit v2 on v1

--- a/solution.py
+++ b/solution.py
@@ -171,11 +171,6 @@
 
     lax.fori_loop(0, cuts, own, 0)
 
-    def finish(k):
-        for side in range(2):
-            back(side, k).wait()
-            contract(piece(side, k), returned, piece(side, k) - cuts)
-
     def travelling(k, carry):
         for side in range(2):
             go(side, k).wait_recv()
@@ -187,15 +182,9 @@
                 shared(step, j).wait_recv()
             apply(j)
             back(side, k).start()
-
-        @pl.when(k > 0)
-        def _():
-            finish(k - 1)
-
         return carry
 
     lax.fori_loop(0, cuts, travelling, 0)
-    finish(cuts - 1)
 
     def drain(j, carry):
         for step in range(1, shares):
@@ -206,25 +195,42 @@
             total = partial[pair, at(me, out_rows)]
             for step in range(1, shares):
                 total += others[step - 1, pair]
-            out[pair] = total * prefactor
-        return carry
-
-    lax.fori_loop(0, 3 * cuts, drain, 0)
+            out[pair] = total
+        return carry
+
+    lax.fori_loop(0, cuts, drain, 0)
     for k in range(cuts):
         for side in range(2):
             go(side, k).wait_send()
+
+    def finish(k, carry):
+        for side in range(2):
+            j = piece(side, k)
+            back(side, k).wait()
+            contract(j, returned, j - cuts)
+
+        @pl.when(k > 0)
+        def _():
+            for side in range(2):
+                drain(piece(side, k - 1), carry)
+
+        return carry
+
+    lax.fori_loop(0, cuts, finish, 0)
+    for side in range(2):
+        drain(piece(side, cuts - 1), 0)
 
 
 def shards(owners, shares, pair_conduction, pair_valence, screened, sphere_sizes):
     count, bands, slab = pair_valence.shape
     gvectors = screened.shape[2]
-    cuts = 4
+    cuts = count // 3
     out_rows = pair_conduction.shape[1] // shares
     rows = count * bands
     dtype = pair_valence.dtype
     dma = pltpu.SemaphoreType.DMA
     anywhere = pl.BlockSpec(memory_space=pl.ANY)
-    return pl.pallas_call(
+    summed = pl.pallas_call(
         functools.partial(kernel, owners, shares, cuts, bands),
         out_shape=jax.ShapeDtypeStruct((count, out_rows, bands), jnp.float32),
         in_specs=[pl.BlockSpec(memory_space=pltpu.SMEM), anywhere, anywhere, anywhere],
@@ -248,7 +254,7 @@
             dma((shares - 1, 3 * cuts)),
         ],
         compiler_params=pltpu.CompilerParams(
-            collective_id=0, has_side_effects=True, vmem_limit_bytes=58 * 1024 * 1024
+            collective_id=0, has_side_effects=True, vmem_limit_bytes=50 * 1024 * 1024
         ),
         cost_estimate=pl.CostEstimate(
             flops=2 * rows * slab * gvectors + 2 * rows * bands * slab,
@@ -261,6 +267,7 @@
         pair_valence.reshape(rows, slab),
         screened.reshape(slab, gvectors),
     )
+    return summed * prefactor
 
 
 def solution(mesh):

time: 192 us -> 190 us (0.990)
  Pallas kernels: 190 us -> 188 us
where the time goes in v2:
time: 190 us
  Pallas kernels  188 us (99%)
    pallas_call x1, Pallas kernels, shards(): pl.pallas_call(functools.partial(kernel, owners, shares, cuts, bands), ou...  188 us

profile of v2, /device:TPU:0, one launch (start us, length us, event | category | flops | bytes accessed | tf_op | source)
XLA Modules:
  0.0 189.6 jit_solution(9090355347421217546)
XLA Ops:
  0.0 0.0 copy-start
  0.0 0.7 copy-done
  0.7 188.1 %shard_map.46 = f32[24,32,64]{2,1,0:T(8,128)S(1)} custom-call(s32[16]{0:T(128)S(1)} %copy-done, bf16[1536,2048]{1,0:T(8,128)(2,1)} %bitcast.4, bf16[1536,2048]{1,0:T(8,128)(2,1)} %bitcast.5, bf16[2048,4096]{1,0:T(8,128)(2,1)} %bitcast.3), custom_call_target="tpu_custom_call" | custom-call | flops 26172456960 | bytes 29360128 | tf_op jit(solution)/shard_map/pallas_call | solution.py:233
  188.8 0.8 broadcast_multiply_fusion
Async XLA Ops:
  0.0 0.7 copy-start
